TPU v7x, 32 devices: a whole 2x2x4 slice. The times are simulated.
32 devices in a mesh: group: 2 (over y), ctx: 4 (over z), head: 2 (over x), sub: 2 (over core).
Axes of the slice: x: 2, y: 2, z: 4, core: 2. Of those that a mesh axis runs over, the one named last changes fastest.
Arguments:
- q_lin: bfloat16 [2048, 32, 128], P(('group', 'ctx'), ('head', 'sub')), parts along dimension 0, may hold values from -1.796875 to 1.796875
- k_lin: bfloat16 [2048, 32, 128], P(('group', 'ctx'), ('head', 'sub')), parts along dimension 0, may hold values from -1.796875 to 1.796875
- v_lin: bfloat16 [2048, 32, 128], P(('group', 'ctx'), ('head', 'sub')), parts along dimension 0, may hold values from -6 to 6
- decay_log: float32 [2048, 32], P(('group', 'ctx'), ('head', 'sub')), parts along dimension 0, may hold values from -0.7 to 0, as said below
- q_soft: bfloat16 [2048, 32, 128], P(('group', 'ctx'), ('head', 'sub')), parts along dimension 0, may hold values from -8 to 8, as said below
- k_soft: bfloat16 [2048, 8, 128], P(('group', 'ctx'), ('head', 'sub')), parts along dimension 0, may hold values from -8 to 8, as said below
- v_soft: bfloat16 [2048, 8, 128], P(('group', 'ctx'), ('head', 'sub')), parts along dimension 0, may hold values from -6 to 6
- doc_starts: int32 [12], P('group'), parts along dimension 0, may hold values from 0 to 768, as said below
Outputs:
- lin_out: bfloat16 [2048, 32, 128], P(('group', 'ctx'), ('head', 'sub')), parts along dimension 0
- soft_out: bfloat16 [2048, 32, 128], P(('group', 'ctx'), ('head', 'sub')), parts along dimension 0
There are 2 independent parts, one for each index of `group`. A program takes and returns all parts, laid end to end along the dimension named above; each array names one. Nothing has to cross between parts.
Inputs may be any that keep to these rules, and one draw needn't show every extreme that they name: `decay_log`: entries are negative. `q_soft`: entries are at most 8 in magnitude. `k_soft`: entries are at most 8 in magnitude. `doc_starts`: starts never fall and are multiples of 256; equal starts (empty documents) may occur. The first is 0, the last is 768, and all others lie at or after position (3) * 256.
All inputs are finite; a program needn't handle non-finite values.
Results may differ from a plain program's by a relative error of at most 0.0075.
Values may be sent and summed in bfloat16 or wider, within the bound.
A program may use at most 64 MiB of HBM per device.

v0:
```python
import math

import jax
import jax.numpy as jnp
from jax import lax
from jax.sharding import PartitionSpec as P


def carried_in(shard, axis, combine, identity):
    size, index = (lax.axis_size(axis), lax.axis_index(axis))
    everything = jax.tree.map(
        lambda part, kind: lax.all_gather(part.astype(kind), axis),
        shard,
        (jnp.bfloat16, jnp.bfloat16),
    )
    start = jax.tree.map(
        lambda part, zero: jnp.broadcast_to(jnp.asarray(zero, part.dtype), part.shape),
        shard,
        identity,
    )

    def step(k, before):
        reached = k < index
        new = combine(
            before, jax.tree.map(lambda part, own: part[k].astype(own.dtype), everything, shard)
        )
        return jax.tree.map(lambda a, b: jnp.where(reached, a, b), new, before)

    return lax.fori_loop(0, size, step, start)


def from_behind(value, axis, steps):
    count = lax.axis_size(axis)
    leading, last = (max(0, -steps), min(count, count - steps))
    return lax.ppermute(value, axis, [(source, source + steps) for source in range(leading, last)])


def doc_index(slice_locations, doc_starts):
    return jnp.sum((doc_starts[None, :] <= slice_locations[:, None]).astype(jnp.int32), axis=1) - 1


def chain_join(earlier, later):
    return (earlier[0] * later[0], earlier[1] * later[0][..., None, None] + later[1])


def lightning_part(q_lin, k_lin, v_lin, decay_log):
    rise = jnp.cumsum(decay_log, axis=0)
    scores = jnp.einsum("ihd,jhd->hij", q_lin, k_lin, preferred_element_type=jnp.float32)
    rows = jnp.arange(q_lin.shape[0])
    lower = (rows[:, None] >= rows[None, :])[None]
    gap = rise.T[:, :, None] - rise.T[:, None, :]
    fade = jnp.where(lower, jnp.exp(jnp.where(lower, gap, 0.0)), 0.0)
    inner = (scores * fade).astype(jnp.bfloat16)
    intra = jnp.einsum("hij,jhd->ihd", inner, v_lin, preferred_element_type=jnp.float32)
    block_decay = rise[-1]
    tail = (k_lin.astype(jnp.float32) * jnp.exp(block_decay[None, :] - rise)[:, :, None]).astype(
        jnp.bfloat16
    )
    local_state = jnp.einsum("jhd,jhe->hde", tail, v_lin, preferred_element_type=jnp.float32)
    return (rise, intra, block_decay, local_state)


def on_device(q_lin, k_lin, v_lin, decay_log, q_soft, k_soft, v_soft, doc_starts):
    rise, intra, block_decay, local_state = lightning_part(q_lin, k_lin, v_lin, decay_log)
    me = lax.axis_index("ctx")
    tok = q_soft.shape[0]
    ranks = lax.axis_size("ctx")
    bounds = doc_index(jnp.stack([me * tok, (me + 1) * tok]), doc_starts)
    keep_next = bounds[0] == bounds[1]
    factor = jnp.where(keep_next, jnp.exp(block_decay), jnp.zeros_like(block_decay))
    addend = jnp.where(keep_next, local_state, jnp.zeros_like(local_state))
    empty = (jnp.ones_like(block_decay), jnp.zeros_like(local_state))
    carried = carried_in((factor, addend), "ctx", chain_join, empty)
    state_in = carried[1]
    lead = q_lin.astype(jnp.float32) * jnp.exp(rise)[:, :, None]
    inter = jnp.einsum("ihd,hde->ihe", lead, state_in, precision=lax.Precision.HIGHEST)
    total = intra + inter
    lin_out = (total * lax.rsqrt(jnp.mean(total * total, axis=-1, keepdims=True) + 1e-06)).astype(
        jnp.bfloat16
    )
    kv_heads = k_soft.shape[1]
    group = q_soft.shape[1] // kv_heads
    head_dim = q_soft.shape[2]
    scale = 1.0 / math.sqrt(head_dim)
    q_pos = me * tok + jnp.arange(tok, dtype=jnp.int32)
    q_doc = doc_index(q_pos, doc_starts)
    q_four = q_soft.reshape(tok, kv_heads, group, head_dim)

    def tile(carry, k_tile, v_tile, k_start):
        k_pos = k_start + jnp.arange(k_tile.shape[0], dtype=jnp.int32)
        k_doc = doc_index(k_pos, doc_starts)
        allowed = (k_pos[None, :] <= q_pos[:, None]) & (k_doc[None, :] == q_doc[:, None])
        top, summed, acc = carry
        scores = (
            jnp.einsum("tkgd,skd->tkgs", q_four, k_tile, preferred_element_type=jnp.float32) * scale
        )
        scores = jnp.where(allowed[:, None, None, :], scores, -jnp.inf)
        new_top = jnp.maximum(top, jnp.max(scores, axis=-1))
        shrink = jnp.exp(top - new_top)
        weights = jnp.exp(scores - new_top[..., None])
        summed = summed * shrink + jnp.sum(weights, axis=-1)
        acc = acc * shrink[..., None] + jnp.einsum(
            "tkgs,skd->tkgd",
            weights.astype(jnp.bfloat16),
            v_tile,
            preferred_element_type=jnp.float32,
        )
        return (new_top, summed, acc)

    initial = (
        jnp.full((tok, kv_heads, group), -1e30, jnp.float32),
        jnp.zeros((tok, kv_heads, group), jnp.float32),
        jnp.zeros((tok, kv_heads, group, head_dim), jnp.float32),
    )
    first = tile(initial, k_soft, v_soft, me * tok)

    def passing(step, state):
        carry, k_held, v_held = state
        k_held, v_held = from_behind((k_held, v_held), "ctx", 1)
        carry = tile(carry, k_held, v_held, (me - step) * tok)
        return (carry, k_held, v_held)

    final = lax.fori_loop(1, ranks, passing, (first, k_soft, v_soft))
    top, summed, acc = final[0]
    soft_out = (
        (acc / summed[..., None]).reshape(tok, kv_heads * group, head_dim).astype(jnp.bfloat16)
    )
    return (lin_out, soft_out)


def solution(mesh):
    return jax.shard_map(
        on_device,
        mesh=mesh,
        in_specs=(
            P(("group", "ctx"), ("head", "sub"), None),
            P(("group", "ctx"), ("head", "sub"), None),
            P(("group", "ctx"), ("head", "sub"), None),
            P(("group", "ctx"), ("head", "sub")),
            P(("group", "ctx"), ("head", "sub"), None),
            P(("group", "ctx"), ("head", "sub"), None),
            P(("group", "ctx"), ("head", "sub"), None),
            P("group"),
        ),
        out_specs=(
            P(("group", "ctx"), ("head", "sub"), None),
            P(("group", "ctx"), ("head", "sub"), None),
        ),
        check_vma=False,
    )
```

profile of v0, /device:TPU:0, one launch (start us, length us, event | category | flops | bytes accessed | tf_op | source)
XLA Modules:
  0.0 88.5 jit_solution(816197125442971011)
XLA Ops:
  7.2 0.0 copy-start
  7.2 0.0 all-gather.4.cloned.1.call-start
  7.3 0.1 pad_add_fusion
  7.3 0.9 %fusion.34 = s32[2]{0:T(128)S(1)} fusion(s32[6]{0:T(128)} %param.19, s32[2]{0:T(128)S(1)} %pad_add_fusion), kind=kLoop, calls=%fused_computation.65 | loop fusion | flops 34 | bytes 40 | tf_op jit(solution)/shard_map/reduce_sum | solution.py:39
  8.3 0.6 fusion.39
  8.9 1.2 %reduce-window.6 = f32[8,2,128]{2,0,1:T(8,128)S(1)} reduce-window(f32[8,2,128]{2,0,1:T(8,128)} %bitcast.102, f32[]{:T(128)} %constant.111.clone.1), window={size=1x1x128 pad=0_0x0_0x127_0}, to_apply=%region_0.0 | reduce-window | flops 260096 | bytes 16388 | tf_op jit(solution)/shard_map/reduce-window
  10.1 0.2 slice_reduce_fusion
  10.3 0.1 fusion.37
  10.4 0.2 slice_reduce_fusion.1
  10.6 0.1 subtract_exponential_fusion.3
  10.6 0.1 copy.82
  12.1 1.4 %multiply_convert_fusion.2 = bf16[256,8,128]{2,1,0:T(8,128)(2,1)S(1)} fusion(bf16[256,8,128]{2,1,0:T(8,128)(2,1)} %param.13, f32[256,8]{1,0:T(8,128)S(1)} %copy.82), kind=kLoop, calls=%fused_computation.39 | loop fusion | flops 786432 | bytes 1056768 | tf_op jit(solution)/shard_map/convert_element_type | solution.py:56
  13.5 1.1 %fusion.16 = bf16[8,128,128]{2,1,0:T(8,128)(2,1)} fusion(bf16[256,8,128]{2,1,0:T(8,128)(2,1)S(1)} %multiply_convert_fusion.2, bf16[256,8,128]{2,1,0:T(8,128)(2,1)S(1)} %copy-done, pred[]{:T(512)} %bitcast.6), kind=kOutput, calls=%fused_computation.32 | convolution fusion | flops 67371008 | bytes 1310721 | tf_op jit(solution)/shard_map/jhd,jhe->hde/dot_general | solution.py:59
  14.6 0.0 all-gather.4.cloned.1.call-update
  14.6 0.2 fusion.33
  14.8 0.1 convert_reduce_fusion.1
  14.9 0.1 compare_and_fusion.1
  15.1 0.1 copy.88
  15.2 0.5 fusion.40
  15.7 0.3 fusion.11
  16.0 0.1 copy-done.2
  16.1 12.5 %all-gather.1 = bf16[4,1,8]{2,1,0:T(2,128)(2,1)S(1)} all-gather(bf16[1,1,8]{2,1,0:T(2,128)(2,1)S(1)} %bitcast.103), channel_id=1, replica_groups=mesh['group'=2,'ctx'=4,'head'=2,'sub'=2] {'ctx'}, dimensions={0}, use_global_device_ids=true | all-gather | bytes 80 | tf_op jit(solution)/shard_map/all_gather | solution.py:12
  28.7 0.9 fusion.14
  29.6 40.8 %while.38 = (s32[]{:T(128)}, f32[256,2,4]{0,2,1:T(4,128)S(1)}, f32[256,2,4]{0,2,1:T(4,128)S(1)}, f32[256,2,4,128]{3,0,2,1:T(8,128)S(1)}, bf16[256,2,128]{2,0,1:T...) while((s32[]{:T(128)}, f32[256,2,4]{0,2,1:T(4,128)S(1)}, ...), condition=%wide.region_13.14_spmd.clone, body=%wide.region_9.13_spmd.clone.sunk | while | flops 272835584 | bytes 11020549 | solution.py:123
  29.6 1.3 %collective-permute-start = (bf16[256,2,128]{2,0,1:T(8,128)(2,1)S(1)}, bf16[256,2,128]{2,0,1:T(8,128)(2,1)S(1)}, u32[]{:S(2)}, u32[]{:S(2)}) collective-permute-start(bf16[256,2,128]{2,0,1:T(8,128)(2,1)S(1)} %get-tuple-element.666), channel_id=1, source_target_pairs={{0,4},{4,8},{8,12},{1,5},{5,9},{9,13},{2,6},{6,10},{10,14},{3,7},{... | collective-permute-start | bytes 393224 | tf_op jit(solution)/shard_map/while/body/eval_jaxpr/ppermute | solution.py:35
  30.9 2.7 %collective-permute-start.1 = (bf16[256,2,128]{2,0,1:T(8,128)(2,1)S(1)}, bf16[256,2,128]{2,0,1:T(8,128)(2,1)S(1)}, u32[]{:S(2)}, u32[]{:S(2)}) collective-permute-start(bf16[256,2,128]{2,0,1:T(8,128)(2,1)S(1)} %get-tuple-element.667), channel_id=1, source_target_pairs={{0,4},{4,8},{8,12},{1,5},{5,9},{9,13},{2,6},{6,10},{10,14},{3,7},{... | collective-permute-start | bytes 393224 | tf_op jit(solution)/shard_map/while/body/eval_jaxpr/ppermute | solution.py:35
  33.6 0.1 convert_reduce_fusion.3
  33.7 0.1 compare_and_fusion.3
  33.9 3.6 %collective-permute-done = bf16[256,2,128]{2,0,1:T(8,128)(2,1)S(1)} collective-permute-done((bf16[256,2,128]{2,0,1:T(8,128)(2,1)S(1)}, bf16[256,2,128]{2,0,1:T(8,128)(2,1)S(1)}, u32[]{:S(2)}, u32[]{:S(2)}) %collective-permute-start) | collective-permute-done | bytes 131104 | tf_op jit(solution)/shard_map/while/body/eval_jaxpr/ppermute | solution.py:35
  37.5 0.5 fusion.54
  38.0 0.3 fusion.55
  38.3 3.8 %collective-permute-done.1 = bf16[256,2,128]{2,0,1:T(8,128)(2,1)S(1)} collective-permute-done((bf16[256,2,128]{2,0,1:T(8,128)(2,1)S(1)}, bf16[256,2,128]{2,0,1:T(8,128)(2,1)S(1)}, u32[]{:S(2)}, u32[]{:S(2)}) %collective-permute-start.1) | collective-permute-done | bytes 131104 | tf_op jit(solution)/shard_map/while/body/eval_jaxpr/ppermute | solution.py:35
  42.2 0.9 %fusion.56 = f32[256,2,4,128]{3,0,2,1:T(8,128)S(1)} fusion(f32[256,2,4,256]{0,3,2,1:T(8,128)S(1)} %get-tuple-element.620, f32[256,2,4,128]{3,0,2,1:T(8,128)S(1)} %get-tuple-element.665, f32[256,2,4]{0,2,1:T(4,128)S(1)} %max.12, f32[256,2,4]{0,2,1:T(4,128)S(1)} %bitcast.95, bf16[256,2,128]{2,0,1:T(8,128)(2,1)S(1)} %collective-permute-done.1), kind=kOutput, calls=%fused_computation.6.clone.1 | convolution fusion | flops 135790592 | bytes 4341760 | tf_op jit(solution)/shard_map/while/body/eval_jaxpr/tkgs,skd->tkgd/dot_general | solution.py:102
  43.1 7.7 %collective-permute-start = (bf16[256,2,128]{2,0,1:T(8,128)(2,1)S(1)}, bf16[256,2,128]{2,0,1:T(8,128)(2,1)S(1)}, u32[]{:S(2)}, u32[]{:S(2)}) collective-permute-start(bf16[256,2,128]{2,0,1:T(8,128)(2,1)S(1)} %get-tuple-element.666), channel_id=1, source_target_pairs={{0,4},{4,8},{8,12},{1,5},{5,9},{9,13},{2,6},{6,10},{10,14},{3,7},{... | collective-permute-start | bytes 393224 | tf_op jit(solution)/shard_map/while/body/eval_jaxpr/ppermute | solution.py:35
  50.8 5.4 %collective-permute-start.1 = (bf16[256,2,128]{2,0,1:T(8,128)(2,1)S(1)}, bf16[256,2,128]{2,0,1:T(8,128)(2,1)S(1)}, u32[]{:S(2)}, u32[]{:S(2)}) collective-permute-start(bf16[256,2,128]{2,0,1:T(8,128)(2,1)S(1)} %get-tuple-element.667), channel_id=1, source_target_pairs={{0,4},{4,8},{8,12},{1,5},{5,9},{9,13},{2,6},{6,10},{10,14},{3,7},{... | collective-permute-start | bytes 393224 | tf_op jit(solution)/shard_map/while/body/eval_jaxpr/ppermute | solution.py:35
  56.3 0.1 convert_reduce_fusion.3
  56.4 0.1 compare_and_fusion.3
  56.6 0.5 fusion.54
  57.0 0.3 fusion.55
  57.4 1.4 %collective-permute-done.1 = bf16[256,2,128]{2,0,1:T(8,128)(2,1)S(1)} collective-permute-done((bf16[256,2,128]{2,0,1:T(8,128)(2,1)S(1)}, bf16[256,2,128]{2,0,1:T(8,128)(2,1)S(1)}, u32[]{:S(2)}, u32[]{:S(2)}) %collective-permute-start.1) | collective-permute-done | bytes 131104 | tf_op jit(solution)/shard_map/while/body/eval_jaxpr/ppermute | solution.py:35
  58.8 0.9 %fusion.56 = f32[256,2,4,128]{3,0,2,1:T(8,128)S(1)} fusion(f32[256,2,4,256]{0,3,2,1:T(8,128)S(1)} %get-tuple-element.620, f32[256,2,4,128]{3,0,2,1:T(8,128)S(1)} %get-tuple-element.665, f32[256,2,4]{0,2,1:T(4,128)S(1)} %max.12, f32[256,2,4]{0,2,1:T(4,128)S(1)} %bitcast.95, bf16[256,2,128]{2,0,1:T(8,128)(2,1)S(1)} %collective-permute-done.1), kind=kOutput, calls=%fused_computation.6.clone.1 | convolution fusion | flops 135790592 | bytes 4341760 | tf_op jit(solution)/shard_map/while/body/eval_jaxpr/tkgs,skd->tkgd/dot_general | solution.py:102
  59.8 4.4 %collective-permute-start = (bf16[256,2,128]{2,0,1:T(8,128)(2,1)S(1)}, bf16[256,2,128]{2,0,1:T(8,128)(2,1)S(1)}, u32[]{:S(2)}, u32[]{:S(2)}) collective-permute-start(bf16[256,2,128]{2,0,1:T(8,128)(2,1)S(1)} %get-tuple-element.666), channel_id=1, source_target_pairs={{0,4},{4,8},{8,12},{1,5},{5,9},{9,13},{2,6},{6,10},{10,14},{3,7},{... | collective-permute-start | bytes 393224 | tf_op jit(solution)/shard_map/while/body/eval_jaxpr/ppermute | solution.py:35
  64.1 2.7 %collective-permute-start.1 = (bf16[256,2,128]{2,0,1:T(8,128)(2,1)S(1)}, bf16[256,2,128]{2,0,1:T(8,128)(2,1)S(1)}, u32[]{:S(2)}, u32[]{:S(2)}) collective-permute-start(bf16[256,2,128]{2,0,1:T(8,128)(2,1)S(1)} %get-tuple-element.667), channel_id=1, source_target_pairs={{0,4},{4,8},{8,12},{1,5},{5,9},{9,13},{2,6},{6,10},{10,14},{3,7},{... | collective-permute-start | bytes 393224 | tf_op jit(solution)/shard_map/while/body/eval_jaxpr/ppermute | solution.py:35
  66.9 0.1 convert_reduce_fusion.3
  67.0 0.1 compare_and_fusion.3
  67.1 0.5 fusion.54
  67.6 0.3 fusion.55
  68.0 1.4 %collective-permute-done.1 = bf16[256,2,128]{2,0,1:T(8,128)(2,1)S(1)} collective-permute-done((bf16[256,2,128]{2,0,1:T(8,128)(2,1)S(1)}, bf16[256,2,128]{2,0,1:T(8,128)(2,1)S(1)}, u32[]{:S(2)}, u32[]{:S(2)}) %collective-permute-start.1) | collective-permute-done | bytes 131104 | tf_op jit(solution)/shard_map/while/body/eval_jaxpr/ppermute | solution.py:35
  69.4 0.9 %fusion.56 = f32[256,2,4,128]{3,0,2,1:T(8,128)S(1)} fusion(f32[256,2,4,256]{0,3,2,1:T(8,128)S(1)} %get-tuple-element.620, f32[256,2,4,128]{3,0,2,1:T(8,128)S(1)} %get-tuple-element.665, f32[256,2,4]{0,2,1:T(4,128)S(1)} %max.12, f32[256,2,4]{0,2,1:T(4,128)S(1)} %bitcast.95, bf16[256,2,128]{2,0,1:T(8,128)(2,1)S(1)} %collective-permute-done.1), kind=kOutput, calls=%fused_computation.6.clone.1 | convolution fusion | flops 135790592 | bytes 4341760 | tf_op jit(solution)/shard_map/while/body/eval_jaxpr/tkgs,skd->tkgd/dot_general | solution.py:102
  70.4 0.3 divide_convert_fusion
  70.7 1.2 %copy.94 = bf16[256,2,4,128]{3,2,1,0:T(4,128)(2,1)} copy(bf16[256,2,4,128]{3,0,2,1:T(8,128)(2,1)S(1)} %divide_convert_fusion) | data formatting | bytes 1048576 | tf_op jit(solution)/shard_map/convert_element_type | solution.py:126
  71.9 0.1 copy.85
  72.1 0.1 add_bitcast_fusion.1
  72.2 0.3 convert_multiply_fusion
  72.5 2.2 %fusion.13 = f32[256,8,128]{0,2,1:T(8,128)S(1)} fusion(f32[8,256]{1,0:T(8,128)S(1)} %add_bitcast_fusion.1, pred[256,256]{1,0:T(8,128)(4,1)S(1)} %iota_compare_fusion, bf16[256,8,128]{2,1,0:T(8,128)(2,1)} %param.13, bf16[256,8,128]{2,1,0:T(8,128)(2,1)} %param.12, bf16[256,8,128]{2,1,0:T(8,128)(2,1)S(1)} %copy-done), kind=kOutput, calls=%fused_computation.26 | convolution fusion | flops 271056896 | bytes 2695168 | tf_op jit(solution)/shard_map/hij,jhd->ihd/dot_general | solution.py:54
  74.7 0.0 all-gather.4.cloned.1.call-done
  74.7 4.5 %while.39 = (s32[]{:T(128)}, f32[8,128,128]{2,1,0:T(8,128)S(1)}, s32[]{:T(128)}, bf16[4,8]{1,0:T(4,128)(2,1)S(1)}, bf16[4,8,128,128]{3,2,1,0:T(8,128)(2,1)}, /*index=5*/s32[]{:T(128)}, s32[]{:T(128)}) while((s32[]{:T(128)}, f32[8,128,128]{2,1,0:T(8,128)S(1)}, s32[]{:T(128)}, bf16[4,8]{1,0:T(4,128)(2,1)S(1)}, ...), condition=%wide.region_4.5_spmd.clone, body=%wide.region_3.4_spmd.clone.sunk | while | flops 655372 | bytes 1310905 | solution.py:29
  74.7 1.1 %fusion.57 = f32[8,128,128]{2,1,0:T(8,128)S(1)} fusion(f32[8,128,128]{2,1,0:T(8,128)S(1)} %get-tuple-element.636, bf16[4,8,128,128]{3,2,1,0:T(8,128)(2,1)} %get-tuple-element.646, s32[]{:T(128)} %get-tuple-element.635, f32[8]{0:T(128)S(1)} %bitcast_convert_fusion.2, pred[]{:T(512)S(6)} %compare.3, pred[]{:T(512)S(6)} %lt.31), kind=kLoop, calls=%fused_computation.18.clone.1 | loop fusion | flops 655360 | bytes 1310758 | tf_op jit(solution)/shard_map/while/body/eval_jaxpr/jit(_where)/select_n | solution.py:27
  75.9 1.1 %fusion.57 = f32[8,128,128]{2,1,0:T(8,128)S(1)} fusion(f32[8,128,128]{2,1,0:T(8,128)S(1)} %get-tuple-element.636, bf16[4,8,128,128]{3,2,1,0:T(8,128)(2,1)} %get-tuple-element.646, s32[]{:T(128)} %get-tuple-element.635, f32[8]{0:T(128)S(1)} %bitcast_convert_fusion.2, pred[]{:T(512)S(6)} %compare.3, pred[]{:T(512)S(6)} %lt.31), kind=kLoop, calls=%fused_computation.18.clone.1 | loop fusion | flops 655360 | bytes 1310758 | tf_op jit(solution)/shard_map/while/body/eval_jaxpr/jit(_where)/select_n | solution.py:27
  77.0 1.1 %fusion.57 = f32[8,128,128]{2,1,0:T(8,128)S(1)} fusion(f32[8,128,128]{2,1,0:T(8,128)S(1)} %get-tuple-element.636, bf16[4,8,128,128]{3,2,1,0:T(8,128)(2,1)} %get-tuple-element.646, s32[]{:T(128)} %get-tuple-element.635, f32[8]{0:T(128)S(1)} %bitcast_convert_fusion.2, pred[]{:T(512)S(6)} %compare.3, pred[]{:T(512)S(6)} %lt.31), kind=kLoop, calls=%fused_computation.18.clone.1 | loop fusion | flops 655360 | bytes 1310758 | tf_op jit(solution)/shard_map/while/body/eval_jaxpr/jit(_where)/select_n | solution.py:27
  78.1 1.1 %fusion.57 = f32[8,128,128]{2,1,0:T(8,128)S(1)} fusion(f32[8,128,128]{2,1,0:T(8,128)S(1)} %get-tuple-element.636, bf16[4,8,128,128]{3,2,1,0:T(8,128)(2,1)} %get-tuple-element.646, s32[]{:T(128)} %get-tuple-element.635, f32[8]{0:T(128)S(1)} %bitcast_convert_fusion.2, pred[]{:T(512)S(6)} %compare.3, pred[]{:T(512)S(6)} %lt.31), kind=kLoop, calls=%fused_computation.18.clone.1 | loop fusion | flops 655360 | bytes 1310758 | tf_op jit(solution)/shard_map/while/body/eval_jaxpr/jit(_where)/select_n | solution.py:27
  79.2 1.2 %multiply_reduce_fusion = (f32[256,8]{0,1:T(8,128)S(1)}, f32[256,8,128]{0,2,1:T(8,128)S(1)}) fusion(f32[256,8,128]{0,2,1:T(8,128)S(1)} %fusion.13, f32[8,128,128]{2,1,0:T(8,128)S(1)} %get-tuple-element.361, f32[256,8,128]{2,1,0:T(8,128)S(1)} %convert_multiply_fusion), kind=kOutput, calls=%fused_computation.37 | convolution fusion | flops 403437568 | bytes 3678208 | tf_op jit(solution)/shard_map/ihd,hde->ihe/dot_general | solution.py:76
  80.5 0.1 multiply_convert_fusion.1
  80.6 1.1 %copy.95 = bf16[256,8,128]{2,1,0:T(8,128)(2,1)} copy(bf16[256,8,128]{0,2,1:T(8,128)(2,1)S(1)} %multiply_convert_fusion.1) | data formatting | bytes 1048576
  (53 shorter events, 0.4 us)
Async XLA Ops:
  7.2 6.4 %copy-start = (bf16[256,8,128]{2,1,0:T(8,128)(2,1)S(1)}, bf16[256,8,128]{2,1,0:T(8,128)(2,1)}, u32[]{:S(2)}) copy-start(bf16[256,8,128]{2,1,0:T(8,128)(2,1)} %param.14) | copy-start | bytes 1572868
  7.2 7.6 %copy-start.5 = (s32[6]{0:T(128)S(1)}, s32[6]{0:T(128)}, u32[]{:S(2)}) copy-start(s32[6]{0:T(128)} %param.19) | copy-start | bytes 76
  7.2 7.9 %copy-start.3 = (bf16[256,8,128]{2,1,0:T(8,128)(2,1)S(1)}, bf16[256,8,128]{2,1,0:T(8,128)(2,1)}, u32[]{:S(2)}) copy-start(bf16[256,8,128]{2,1,0:T(8,128)(2,1)} %param.16) | copy-start | bytes 1572868
  7.2 67.5 %all-gather.4.cloned.1.call-start = ((), (), s32[]{:S(2)}) async-start(), calls=%async_computation | async-start | bytes 1310720 | tf_op jit(solution)/shard_map/all_gather | solution.py:12
  12.1 3.1 %copy-start.1 = (bf16[256,2,128]{2,1,0:T(2,128)(2,1)S(1)}, bf16[256,2,128]{2,1,0:T(2,128)(2,1)}, u32[]{:S(2)}) copy-start(bf16[256,2,128]{2,1,0:T(2,128)(2,1)} %param.17) | copy-start | bytes 393220
  15.2 0.9 %copy-start.2 = (bf16[256,2,128]{2,1,0:T(2,128)(2,1)S(1)}, bf16[256,2,128]{2,1,0:T(2,128)(2,1)}, u32[]{:S(2)}) copy-start(bf16[256,2,128]{2,1,0:T(2,128)(2,1)} %param.18) | copy-start | bytes 393220
  29.6 7.9 %collective-permute-start = (bf16[256,2,128]{2,0,1:T(8,128)(2,1)S(1)}, bf16[256,2,128]{2,0,1:T(8,128)(2,1)S(1)}, u32[]{:S(2)}, u32[]{:S(2)}) collective-permute-start(bf16[256,2,128]{2,0,1:T(8,128)(2,1)S(1)} %get-tuple-element.666), channel_id=1, source_target_pairs={{0,4},{4,8},{8,12},{1,5},{5,9},{9,13},{2,6},{6,10},{10,14},{3,7},{... | collective-permute-start | bytes 393224 | tf_op jit(solution)/shard_map/while/body/eval_jaxpr/ppermute | solution.py:35
  30.9 11.3 %collective-permute-start.1 = (bf16[256,2,128]{2,0,1:T(8,128)(2,1)S(1)}, bf16[256,2,128]{2,0,1:T(8,128)(2,1)S(1)}, u32[]{:S(2)}, u32[]{:S(2)}) collective-permute-start(bf16[256,2,128]{2,0,1:T(8,128)(2,1)S(1)} %get-tuple-element.667), channel_id=1, source_target_pairs={{0,4},{4,8},{8,12},{1,5},{5,9},{9,13},{2,6},{6,10},{10,14},{3,7},{... | collective-permute-start | bytes 393224 | tf_op jit(solution)/shard_map/while/body/eval_jaxpr/ppermute | solution.py:35
  43.1 13.4 %collective-permute-start = (bf16[256,2,128]{2,0,1:T(8,128)(2,1)S(1)}, bf16[256,2,128]{2,0,1:T(8,128)(2,1)S(1)}, u32[]{:S(2)}, u32[]{:S(2)}) collective-permute-start(bf16[256,2,128]{2,0,1:T(8,128)(2,1)S(1)} %get-tuple-element.666), channel_id=1, source_target_pairs={{0,4},{4,8},{8,12},{1,5},{5,9},{9,13},{2,6},{6,10},{10,14},{3,7},{... | collective-permute-start | bytes 393224 | tf_op jit(solution)/shard_map/while/body/eval_jaxpr/ppermute | solution.py:35
  50.8 7.9 %collective-permute-start.1 = (bf16[256,2,128]{2,0,1:T(8,128)(2,1)S(1)}, bf16[256,2,128]{2,0,1:T(8,128)(2,1)S(1)}, u32[]{:S(2)}, u32[]{:S(2)}) collective-permute-start(bf16[256,2,128]{2,0,1:T(8,128)(2,1)S(1)} %get-tuple-element.667), channel_id=1, source_target_pairs={{0,4},{4,8},{8,12},{1,5},{5,9},{9,13},{2,6},{6,10},{10,14},{3,7},{... | collective-permute-start | bytes 393224 | tf_op jit(solution)/shard_map/while/body/eval_jaxpr/ppermute | solution.py:35
  59.8 7.4 %collective-permute-start = (bf16[256,2,128]{2,0,1:T(8,128)(2,1)S(1)}, bf16[256,2,128]{2,0,1:T(8,128)(2,1)S(1)}, u32[]{:S(2)}, u32[]{:S(2)}) collective-permute-start(bf16[256,2,128]{2,0,1:T(8,128)(2,1)S(1)} %get-tuple-element.666), channel_id=1, source_target_pairs={{0,4},{4,8},{8,12},{1,5},{5,9},{9,13},{2,6},{6,10},{10,14},{3,7},{... | collective-permute-start | bytes 393224 | tf_op jit(solution)/shard_map/while/body/eval_jaxpr/ppermute | solution.py:35
  64.1 5.3 %collective-permute-start.1 = (bf16[256,2,128]{2,0,1:T(8,128)(2,1)S(1)}, bf16[256,2,128]{2,0,1:T(8,128)(2,1)S(1)}, u32[]{:S(2)}, u32[]{:S(2)}) collective-permute-start(bf16[256,2,128]{2,0,1:T(8,128)(2,1)S(1)} %get-tuple-element.667), channel_id=1, source_target_pairs={{0,4},{4,8},{8,12},{1,5},{5,9},{9,13},{2,6},{6,10},{10,14},{3,7},{... | collective-permute-start | bytes 393224 | tf_op jit(solution)/shard_map/while/body/eval_jaxpr/ppermute | solution.py:35
  70.4 1.8 %copy-start.4 = (bf16[256,8,128]{2,1,0:T(8,128)(2,1)S(1)}, bf16[256,8,128]{2,1,0:T(8,128)(2,1)}, u32[]{:S(2)}) copy-start(bf16[256,8,128]{2,1,0:T(8,128)(2,1)} %param.12) | copy-start | bytes 1572868
Sparse Core Ops, SparseCore 0:
  14.7 33.8 all-gather.3
where the time goes:
time: 89 us; the launch traced here: 88.5 us
  starting transfers between devices  24.3 us (27%)
  between operations  15.6 us (18%)
  blocking collectives  12.5 us (14%)
  other arithmetic  11.6 us (13%)
  waiting for transfers between devices  10.3 us (12%)
  matrix products  10 us (11%)
  local copies, waits for them, and re-layouts  3.77 us (4%)
    ppermute x6, starting transfers between devices, from_behind(): lax.ppermute(value, axis, [(source, source + steps) for source in range(l...  24.3 us
    all_gather x1, blocking collectives, carried_in(): lax.all_gather(part.astype(kind), axis)  12.5 us
    ppermute x6, waiting for transfers between devices, from_behind(): lax.ppermute(value, axis, [(source, source + steps) for source in range(l...  10.3 us
    select_n x4, other arithmetic, step(): return jax.tree.map(lambda a, b: jnp.where(reached, a, b), new, before)  4.37 us
    dot_general x4, matrix products, tile(): jnp.einsum('tkgs,skd->tkgd', weights.astype(jnp.bfloat16), v_tile, prefer...  3.72 us
    dot_general x1, matrix products, lightning_part(): jnp.einsum('hij,jhd->ihd', inner, v_lin, preferred_element_type=jnp.float32)  2.18 us
    dot_general x4, matrix products, tile(): jnp.einsum('tkgd,skd->tkgs', q_four, k_tile, preferred_element_type=jnp.f...  1.84 us
  transfers between devices with their start and end apart: 7, of which 4 were waited for; matrix products, arithmetic and copies ran while one was open for 14% of the time, Pallas kernels for 0%

commit v1 on v0

v1 whole, which is shorter than its diff:
```python
import functools
import math

import jax
import jax.numpy as jnp
from jax import lax
from jax.experimental import pallas as pl
from jax.experimental.pallas import tpu as pltpu
from jax.sharding import PartitionSpec as P

MESH = pl.DeviceIdType.MESH
F32, BF16 = jnp.float32, jnp.bfloat16
NEVER = -1e30


def dot(a, b, contract):
    return lax.dot_general(a, b, ((contract[:1], contract[1:]), ((), ())), preferred_element_type=F32)


def kernel(n, tok, heads, kv_heads, share, chunk, starts, ql_hbm, kl_hbm, vl_hbm, decay_hbm, qs_hbm, ks_hbm, vs_hbm,
           lin_hbm, soft_hbm,
           ql, kl, vl, decay, qs, ks, vs, lin_out, soft_out,
           k_held, v_held, s_held, s_own, local_state, wide, q_head, k_head, v_head, intra, top, acc,
           in_sems, out_sems, own_sems, pass_sems, kv_sems, s_send, s_recv):
    me = lax.axis_index("ctx")
    sends = me < n - 2
    takes = (me > 0) & (me < n - 1)
    right, left = me + 1, me - 1
    rows, cols = tok * heads, tok * kv_heads

    barrier = pltpu.get_barrier_semaphore()

    @pl.when(sends)
    def _():
        pl.semaphore_signal(barrier, inc=1, device_id={"ctx": right}, device_id_type=MESH)

    @pl.when(takes)
    def _():
        pl.semaphore_signal(barrier, inc=1, device_id={"ctx": left}, device_id_type=MESH)

    loads = [
        pltpu.make_async_copy(src, dst, in_sems.at[i])
        for i, (src, dst) in enumerate(
            [(decay_hbm, decay), (kl_hbm, kl), (vl_hbm, vl), (ql_hbm, ql), (qs_hbm, qs), (ks_hbm, ks), (vs_hbm, vs)]
        )
    ]
    for load in loads:
        load.start()

    @pl.when(sends & takes)
    def _():
        pl.semaphore_wait(barrier, 2)

    @pl.when(sends != takes)
    def _():
        pl.semaphore_wait(barrier, 1)

    def push(src, dst, send_sem, recv_sem):
        return pltpu.make_async_remote_copy(
            src_ref=src, dst_ref=dst, send_sem=send_sem, recv_sem=recv_sem,
            device_id={"ctx": right}, device_id_type=MESH,
        )

    def own_pushes():
        return (
            push(ks_hbm, k_held.at[me], own_sems.at[0], kv_sems.at[me, 0]),
            push(vs_hbm, v_held.at[me], own_sems.at[1], kv_sems.at[me, 1]),
        )

    def passes(slot):
        return (
            push(k_held.at[slot], k_held.at[slot], pass_sems.at[slot, 0], kv_sems.at[slot, 0]),
            push(v_held.at[slot], v_held.at[slot], pass_sems.at[slot, 1], kv_sems.at[slot, 1]),
        )

    def state_push(c):
        part = pl.ds(c * chunk, chunk)
        return push(s_own.at[part], s_held.at[part], s_send.at[c], s_recv.at[c])

    @pl.when(sends)
    def _():
        for copy in own_pushes():
            copy.start()

    def doc_of(position):
        return sum((starts[i] <= position).astype(jnp.int32) for i in range(starts.shape[0]))

    my_doc = doc_of(me * tok)
    keep_next = jnp.where(my_doc == doc_of((me + 1) * tok), 1.0, 0.0).astype(F32)

    loads[0].wait()
    d = decay[...]
    d1 = d.astype(BF16)
    rest = d - d1.astype(F32)
    d2 = rest.astype(BF16)
    d3 = (rest - d2.astype(F32)).astype(BF16)
    i_row = lax.broadcasted_iota(jnp.int32, (tok, tok), 0)
    i_col = lax.broadcasted_iota(jnp.int32, (tok, tok), 1)
    lower = i_row >= i_col
    tri = jnp.where(lower, 1.0, 0.0).astype(BF16)
    rise = dot(tri, d1, (1, 1)) + dot(tri, d2, (1, 1)) + dot(tri, d3, (1, 1))
    rise_t = dot(d1, tri, (1, 1)) + dot(d2, tri, (1, 1)) + dot(d3, tri, (1, 1))
    last = rise[tok - 1 :, :]
    to_end = jnp.exp(last - rise)
    from_start = jnp.exp(rise)
    block_factor = jnp.exp(last)

    def by_head(src, dst):
        wide[...] = src[...].astype(F32)
        for h in range(heads):
            dst[h] = wide[pl.ds(h, tok, stride=heads), :].astype(BF16)

    loads[1].wait()
    by_head(kl, k_head)
    loads[2].wait()
    by_head(vl, v_head)

    @pl.when(sends)
    def _():
        for h in range(heads):
            tail = (k_head[h].astype(F32) * to_end[:, h : h + 1]).astype(BF16)
            local_state[h] = dot(tail, v_head[h], (0, 0))

    @pl.when(me == 0)
    def _():
        for c in range(heads // chunk):
            for h in range(c * chunk, (c + 1) * chunk):
                s_own[h] = (keep_next * local_state[h]).astype(BF16)
            state_push(c).start()

    c2 = math.log2(math.e) / math.sqrt(qs.shape[1])
    tile = min(256, rows)
    part_rows = lax.broadcasted_iota(jnp.int32, (tile, cols), 0)
    part_cols = lax.broadcasted_iota(jnp.int32, (tile, cols), 1)
    ones = jnp.ones((cols, qs.shape[1]), BF16)

    def own_block():
        def step(i, _):
            at = pl.ds(pl.multiple_of(i * tile, tile), tile)
            s = dot(qs[at, :], ks[...], (1, 1))
            fits = (part_rows % heads) // share == part_cols % kv_heads
            past = part_cols // kv_heads <= i * (tile // heads) + part_rows // heads
            s = jnp.where(fits & past, s, NEVER)
            high = jnp.max(s, axis=1, keepdims=True)
            p = jnp.exp2((s - high) * c2).astype(BF16)
            top[at, :] = jnp.broadcast_to(high, (tile, 128))
            acc[at, :] = dot(p, jnp.concatenate([vs[...], ones], axis=1), (1, 0))
            return 0

        lax.fori_loop(0, rows // tile, step, 0)

    def held_block(slot):
        bias = jnp.where(doc_of(slot * tok) == my_doc, 0.0, NEVER).astype(F32)

        def step(i, _):
            at = pl.ds(pl.multiple_of(i * tile, tile), tile)
            s = dot(qs[at, :], k_held[slot], (1, 1))
            fits = (part_rows % heads) // share == part_cols % kv_heads
            s = jnp.where(fits, s + bias, NEVER)
            before = top[at, :]
            high = jnp.maximum(before, jnp.max(s, axis=1, keepdims=True))
            p = jnp.exp2((s - high[:, :1]) * c2).astype(BF16)
            shrink = jnp.exp2((before - high) * c2)
            top[at, :] = high
            acc[at, :] = acc[at, :] * jnp.concatenate([shrink, shrink], axis=1) + dot(
                p, jnp.concatenate([v_held[slot], ones], axis=1), (1, 0)
            )
            return 0

        lax.fori_loop(0, rows // tile, step, 0)

    def arrive(slot):
        for incoming, outgoing in zip(passes(slot), passes(slot)):
            incoming.wait_recv()

            @pl.when(sends)
            def _():
                outgoing.start()

    for load in loads[4:]:
        load.wait()
    own_block()

    @pl.when(takes)
    def _():
        arrive(me - 1)

    loads[3].wait()
    by_head(ql, q_head)
    for h in range(heads):
        gap = jnp.where(lower, rise[:, h : h + 1] - rise_t[h : h + 1, :], NEVER)
        inner = (dot(q_head[h], k_head[h], (1, 1)) * jnp.exp(gap)).astype(BF16)
        intra[h] = dot(inner, v_head[h], (1, 0))

    @pl.when(takes)
    def _():
        held_block(me - 1)

        def step(k, _):
            slot = me - k
            arrive(slot)
            held_block(slot)
            return 0

        lax.fori_loop(2, me + 1, step, 0)

    width = qs.shape[1]
    soft_out[...] = (acc[:, :width] / acc[:, width:]).astype(BF16)
    soft_store = pltpu.make_async_copy(soft_out, soft_hbm, out_sems.at[0])
    soft_store.start()

    def finish(h, total):
        size = jnp.mean(total * total, axis=1, keepdims=True)
        wide[pl.ds(h, tok, stride=heads), :] = total * lax.rsqrt(size + 1e-6)

    @pl.when(takes)
    def _():
        for c in range(heads // chunk):
            state_push(c).wait_recv()

            @pl.when(sends)
            def _():
                for h in range(c * chunk, (c + 1) * chunk):
                    joined = s_held[h].astype(F32) * block_factor[:, h : h + 1] + local_state[h]
                    s_own[h] = (keep_next * joined).astype(BF16)
                state_push(c).start()

            for h in range(c * chunk, (c + 1) * chunk):
                finish(h, intra[h] + from_start[:, h : h + 1] * dot(q_head[h], s_held[h], (1, 0)))

    @pl.when(jnp.logical_not(takes))
    def _():
        for h in range(heads):
            finish(h, intra[h])

    lin_out[...] = wide[...].astype(BF16)
    lin_store = pltpu.make_async_copy(lin_out, lin_hbm, out_sems.at[1])
    lin_store.start()

    @pl.when(sends)
    def _():
        for copy in own_pushes():
            copy.wait_send()
        for c in range(heads // chunk):
            state_push(c).wait_send()

        def step(slot, _):
            for copy in passes(slot):
                copy.wait_send()
            return 0

        lax.fori_loop(0, me, step, 0)

    soft_store.wait()
    lin_store.wait()


def on_device(n, q_lin, k_lin, v_lin, decay_log, q_soft, k_soft, v_soft, doc_starts):
    tok, heads, width = q_lin.shape
    kv_heads = k_soft.shape[1]
    rows, cols, slots = tok * heads, tok * kv_heads, max(n - 2, 1)
    chunk = 2
    flat = lambda x: x.reshape(-1, width)
    hbm = pl.BlockSpec(memory_space=pl.ANY)
    vmem = pltpu.VMEM
    dma = pltpu.SemaphoreType.DMA
    lin, soft = pl.pallas_call(
        functools.partial(kernel, n, tok, heads, kv_heads, q_soft.shape[1] // kv_heads, chunk),
        out_shape=[jax.ShapeDtypeStruct((rows, width), BF16)] * 2,
        in_specs=[pl.BlockSpec(memory_space=pltpu.SMEM)] + [hbm] * 7,
        out_specs=[hbm, hbm],
        scratch_shapes=[
            vmem((rows, width), BF16), vmem((rows, width), BF16), vmem((rows, width), BF16),
            vmem((heads, tok), F32), vmem((rows, width), BF16), vmem((cols, width), BF16), vmem((cols, width), BF16),
            vmem((rows, width), BF16), vmem((rows, width), BF16),
            vmem((slots, cols, width), BF16), vmem((slots, cols, width), BF16),
            vmem((heads, width, width), BF16), vmem((heads, width, width), BF16), vmem((heads, width, width), F32),
            vmem((rows, width), F32),
            vmem((heads, tok, width), BF16), vmem((heads, tok, width), BF16), vmem((heads, tok, width), BF16),
            vmem((heads, tok, width), F32),
            vmem((rows, 128), F32), vmem((rows, 2 * width), F32),
            dma((7,)), dma((2,)), dma((2,)), dma((slots, 2)), dma((slots, 2)),
            dma((heads // chunk,)), dma((heads // chunk,)),
        ],
        compiler_params=pltpu.CompilerParams(
            collective_id=0, has_side_effects=True, vmem_limit_bytes=60 * 1024 * 1024
        ),
        cost_estimate=pl.CostEstimate(flops=2_000_000_000, bytes_accessed=4_000_000, transcendentals=4_000_000),
    )(doc_starts, flat(q_lin), flat(k_lin), flat(v_lin), decay_log.T, flat(q_soft), flat(k_soft), flat(v_soft))
    return lin.reshape(q_lin.shape), soft.reshape(q_soft.shape)


def solution(mesh):
    long = P(("group", "ctx"), ("head", "sub"), None)
    return jax.shard_map(
        functools.partial(on_device, mesh.shape["ctx"]),
        mesh=mesh,
        in_specs=(long, long, long, P(("group", "ctx"), ("head", "sub")), long, long, long, P("group")),
        out_specs=(long, long),
        check_vma=False,
    )
```

time: 89 us -> 27.2 us (0.31)
  the two profiles are of different devices: /device:TPU:0 before, /device:TPU:18 now
where the time goes in v1:
time: 27.2 us; the launch traced here: 27.1 us
  Pallas kernels  23.7 us (87%)
  local copies, waits for them, and re-layouts  2.72 us (10%)
  between operations  0.65 us (2%)
    pallas_call x1, Pallas kernels, on_device(): pl.pallas_call(functools.partial(kernel, n, tok, heads, kv_heads, q_soft....  23.7 us
    unnamed x4, local copies, waits for them, and re-layouts  2.72 us

profile of v1, /device:TPU:18, one launch (start us, length us, event | category | flops | bytes accessed | tf_op | source)
XLA Modules:
  0.0 27.1 jit_solution(7148041984458301861)
XLA Ops:
  0.6 23.7 %shard_map.95 = (bf16[2048,128]{1,0:T(8,128)(2,1)}, bf16[2048,128]{1,0:T(8,128)(2,1)}) custom-call(s32[6]{0:T(128)} %starts.1, bf16[2048,128]{1,0:T(8,128)(2,1)} %bitcast.11, bf16[2048,128]{1,0:T(8,128)(2,1)} %bitcast.12, bf16[2048,128]{1,0:T(8,128)(2,1)} %bitcast.13, f32[8,256]{1,0:T(8,128)} %bitcast.17, bf16[2048,128]{1,0:T(8,128)(2,1)} %bitcast.14, ...), custom_call_target="tpu_custom_call" | custom-call | flops 2000000000 | bytes 4000000 | tf_op jit(solution)/shard_map/pallas_call | solution.py:267
  24.3 0.0 copy-start
  24.3 1.9 %copy.12 = bf16[256,8,128]{2,1,0:T(8,128)(2,1)} copy(bf16[256,8,128]{2,1,0:T(8,128)(2,1)} %bitcast.10) | data formatting | bytes 1048576
  26.3 0.0 copy-done
  26.3 0.8 %copy.13 = bf16[256,8,128]{2,1,0:T(8,128)(2,1)} copy(bf16[256,8,128]{2,1,0:T(8,128)(2,1)S(1)} %bitcast.9) | data formatting | bytes 1048576
Async XLA Ops:
  24.3 1.9 %copy-start = (bf16[2048,128]{1,0:T(8,128)(2,1)S(1)}, bf16[2048,128]{1,0:T(8,128)(2,1)}, u32[]{:S(2)}) copy-start(bf16[2048,128]{1,0:T(8,128)(2,1)} %get-tuple-element.5) | copy-start | bytes 1572868

commit v2 on v1

--- a/solution.py
+++ b/solution.py
@@ -18,10 +18,10 @@
 
 
 def kernel(n, tok, heads, kv_heads, share, chunk, starts, ql_hbm, kl_hbm, vl_hbm, decay_hbm, qs_hbm, ks_hbm, vs_hbm,
-           lin_hbm, soft_hbm,
-           ql, kl, vl, decay, qs, ks, vs, lin_out, soft_out,
+           lin_out, soft_out,
+           ql, kl, vl, decay, qs, ks, vs, q_wide, k_near, v_near,
            k_held, v_held, s_held, s_own, local_state, wide, q_head, k_head, v_head, intra, top, acc,
-           in_sems, out_sems, own_sems, pass_sems, kv_sems, s_send, s_recv):
+           in_sems, own_sems, pass_sems, kv_sems, s_send, s_recv):
     me = lax.axis_index("ctx")
     sends = me < n - 2
     takes = (me > 0) & (me < n - 1)
@@ -128,46 +128,60 @@
                 s_own[h] = (keep_next * local_state[h]).astype(BF16)
             state_push(c).start()
 
-    c2 = math.log2(math.e) / math.sqrt(qs.shape[1])
+    width = qs.shape[1]
+    c2 = math.log2(math.e) / math.sqrt(width)
     tile = min(256, rows)
-    part_rows = lax.broadcasted_iota(jnp.int32, (tile, cols), 0)
-    part_cols = lax.broadcasted_iota(jnp.int32, (tile, cols), 1)
-    ones = jnp.ones((cols, qs.shape[1]), BF16)
+    span = tile // heads
+    head_bits, share_bits = heads.bit_length() - 1, share.bit_length() - 1
+    kv_of_row = (lax.broadcasted_iota(jnp.int32, (tile, width), 0) & (heads - 1)) >> share_bits
+    mine = [jnp.where(kv_of_row == g, 1.0, 0.0).astype(F32) for g in range(kv_heads)]
+
+    def spread(k_ref, v_ref):
+        for src, dst in ((k_ref, k_near), (v_ref, v_near)):
+            wide[pl.ds(0, cols), :] = src[...].astype(F32)
+            for g in range(kv_heads):
+                dst[:, g * width : (g + 1) * width] = wide[pl.ds(g, tok, stride=kv_heads), :].astype(BF16)
+
+    def weigh(p, depth):
+        both = dot(p, v_near[pl.ds(0, depth), :], (1, 0))
+        own = sum(both[:, g * width : (g + 1) * width] * mine[g] for g in range(kv_heads))
+        return own, both[:, kv_heads * width :]
 
     def own_block():
-        def step(i, _):
-            at = pl.ds(pl.multiple_of(i * tile, tile), tile)
-            s = dot(qs[at, :], ks[...], (1, 1))
-            fits = (part_rows % heads) // share == part_cols % kv_heads
-            past = part_cols // kv_heads <= i * (tile // heads) + part_rows // heads
-            s = jnp.where(fits & past, s, NEVER)
+        mask_bf = [m.astype(BF16) for m in mine]
+        for i in range(rows // tile):
+            for g in range(kv_heads):
+                q_wide[pl.ds(i * tile, tile), g * width : (g + 1) * width] = qs[pl.ds(i * tile, tile), :] * mask_bf[g]
+        v_near[:, kv_heads * width :] = jnp.ones((tok, width), BF16)
+        spread(ks, vs)
+        for i in range(rows // tile):
+            at = pl.ds(i * tile, tile)
+            depth = min(tok, -(-(i + 1) * span // width) * width)
+            s = dot(q_wide[at, :], k_near[pl.ds(0, depth), :], (1, 1))
+            token = (lax.broadcasted_iota(jnp.int32, (tile, depth), 0) >> head_bits) + i * span
+            s = jnp.where(lax.broadcasted_iota(jnp.int32, (tile, depth), 1) <= token, s, NEVER)
             high = jnp.max(s, axis=1, keepdims=True)
             p = jnp.exp2((s - high) * c2).astype(BF16)
-            top[at, :] = jnp.broadcast_to(high, (tile, 128))
-            acc[at, :] = dot(p, jnp.concatenate([vs[...], ones], axis=1), (1, 0))
-            return 0
-
-        lax.fori_loop(0, rows // tile, step, 0)
+            top[at, :] = jnp.broadcast_to(high, (tile, width))
+            own, size = weigh(p, depth)
+            acc[at, :width] = own
+            acc[at, width:] = size
 
     def held_block(slot):
         bias = jnp.where(doc_of(slot * tok) == my_doc, 0.0, NEVER).astype(F32)
-
-        def step(i, _):
-            at = pl.ds(pl.multiple_of(i * tile, tile), tile)
-            s = dot(qs[at, :], k_held[slot], (1, 1))
-            fits = (part_rows % heads) // share == part_cols % kv_heads
-            s = jnp.where(fits, s + bias, NEVER)
+        spread(k_held.at[slot], v_held.at[slot])
+
+        for i in range(rows // tile):
+            at = pl.ds(i * tile, tile)
+            s = dot(q_wide[at, :], k_near[...], (1, 1)) + bias
             before = top[at, :]
             high = jnp.maximum(before, jnp.max(s, axis=1, keepdims=True))
             p = jnp.exp2((s - high[:, :1]) * c2).astype(BF16)
             shrink = jnp.exp2((before - high) * c2)
             top[at, :] = high
-            acc[at, :] = acc[at, :] * jnp.concatenate([shrink, shrink], axis=1) + dot(
-                p, jnp.concatenate([v_held[slot], ones], axis=1), (1, 0)
-            )
-            return 0
-
-        lax.fori_loop(0, rows // tile, step, 0)
+            own, size = weigh(p, tok)
+            acc[at, :width] = acc[at, :width] * shrink + own
+            acc[at, width:] = acc[at, width:] * shrink + size
 
     def arrive(slot):
         for incoming, outgoing in zip(passes(slot), passes(slot)):
@@ -187,10 +201,19 @@
 
     loads[3].wait()
     by_head(ql, q_head)
-    for h in range(heads):
-        gap = jnp.where(lower, rise[:, h : h + 1] - rise_t[h : h + 1, :], NEVER)
-        inner = (dot(q_head[h], k_head[h], (1, 1)) * jnp.exp(gap)).astype(BF16)
-        intra[h] = dot(inner, v_head[h], (1, 0))
+    for c in range(heads // chunk):
+        for h in range(c * chunk, (c + 1) * chunk):
+            gap = jnp.where(lower, rise[:, h : h + 1] - rise_t[h : h + 1, :], NEVER)
+            inner = (dot(q_head[h], k_head[h], (1, 1)) * jnp.exp(gap)).astype(BF16)
+            intra[h] = dot(inner, v_head[h], (1, 0))
+
+        @pl.when(takes & sends)
+        def _():
+            state_push(c).wait_recv()
+            for h in range(c * chunk, (c + 1) * chunk):
+                joined = s_held[h].astype(F32) * block_factor[:, h : h + 1] + local_state[h]
+                s_own[h] = (keep_next * joined).astype(BF16)
+            state_push(c).start()
 
     @pl.when(takes)
     def _():
@@ -204,10 +227,7 @@
 
         lax.fori_loop(2, me + 1, step, 0)
 
-    width = qs.shape[1]
     soft_out[...] = (acc[:, :width] / acc[:, width:]).astype(BF16)
-    soft_store = pltpu.make_async_copy(soft_out, soft_hbm, out_sems.at[0])
-    soft_store.start()
 
     def finish(h, total):
         size = jnp.mean(total * total, axis=1, keepdims=True)
@@ -216,14 +236,9 @@
     @pl.when(takes)
     def _():
         for c in range(heads // chunk):
-            state_push(c).wait_recv()
-
-            @pl.when(sends)
+            @pl.when(jnp.logical_not(sends))
             def _():
-                for h in range(c * chunk, (c + 1) * chunk):
-                    joined = s_held[h].astype(F32) * block_factor[:, h : h + 1] + local_state[h]
-                    s_own[h] = (keep_next * joined).astype(BF16)
-                state_push(c).start()
+                state_push(c).wait_recv()
 
             for h in range(c * chunk, (c + 1) * chunk):
                 finish(h, intra[h] + from_start[:, h : h + 1] * dot(q_head[h], s_held[h], (1, 0)))
@@ -234,8 +249,6 @@
             finish(h, intra[h])
 
     lin_out[...] = wide[...].astype(BF16)
-    lin_store = pltpu.make_async_copy(lin_out, lin_hbm, out_sems.at[1])
-    lin_store.start()
 
     @pl.when(sends)
     def _():
@@ -250,9 +263,6 @@
             return 0
 
         lax.fori_loop(0, me, step, 0)
-
-    soft_store.wait()
-    lin_store.wait()
 
 
 def on_device(n, q_lin, k_lin, v_lin, decay_log, q_soft, k_soft, v_soft, doc_starts):
@@ -261,29 +271,30 @@
     rows, cols, slots = tok * heads, tok * kv_heads, max(n - 2, 1)
     chunk = 2
     flat = lambda x: x.reshape(-1, width)
-    hbm = pl.BlockSpec(memory_space=pl.ANY)
+    hbm = pl.BlockSpec(memory_space=pltpu.HBM)
+    near = pl.BlockSpec(memory_space=pltpu.VMEM)
     vmem = pltpu.VMEM
     dma = pltpu.SemaphoreType.DMA
     lin, soft = pl.pallas_call(
         functools.partial(kernel, n, tok, heads, kv_heads, q_soft.shape[1] // kv_heads, chunk),
         out_shape=[jax.ShapeDtypeStruct((rows, width), BF16)] * 2,
         in_specs=[pl.BlockSpec(memory_space=pltpu.SMEM)] + [hbm] * 7,
-        out_specs=[hbm, hbm],
+        out_specs=[near, near],
         scratch_shapes=[
             vmem((rows, width), BF16), vmem((rows, width), BF16), vmem((rows, width), BF16),
             vmem((heads, tok), F32), vmem((rows, width), BF16), vmem((cols, width), BF16), vmem((cols, width), BF16),
-            vmem((rows, width), BF16), vmem((rows, width), BF16),
+            vmem((rows, kv_heads * width), BF16), vmem((tok, kv_heads * width), BF16), vmem((tok, (kv_heads + 1) * width), BF16),
             vmem((slots, cols, width), BF16), vmem((slots, cols, width), BF16),
             vmem((heads, width, width), BF16), vmem((heads, width, width), BF16), vmem((heads, width, width), F32),
             vmem((rows, width), F32),
             vmem((heads, tok, width), BF16), vmem((heads, tok, width), BF16), vmem((heads, tok, width), BF16),
             vmem((heads, tok, width), F32),
-            vmem((rows, 128), F32), vmem((rows, 2 * width), F32),
-            dma((7,)), dma((2,)), dma((2,)), dma((slots, 2)), dma((slots, 2)),
+            vmem((rows, width), F32), vmem((rows, 2 * width), F32),
+            dma((7,)), dma((2,)), dma((slots, 2)), dma((slots, 2)),
             dma((heads // chunk,)), dma((heads // chunk,)),
         ],
         compiler_params=pltpu.CompilerParams(
-            collective_id=0, has_side_effects=True, vmem_limit_bytes=60 * 1024 * 1024
+            collective_id=0, has_side_effects=True, vmem_limit_bytes=32 * 1024 * 1024
         ),
         cost_estimate=pl.CostEstimate(flops=2_000_000_000, bytes_accessed=4_000_000, transcendentals=4_000_000),
     )(doc_starts, flat(q_lin), flat(k_lin), flat(v_lin), decay_log.T, flat(q_soft), flat(k_soft), flat(v_soft))

time: 27.2 us -> 29.7 us (1.092)
  local copies, waits for them, and re-layouts: 2.72 us -> 8.24 us
  Pallas kernels: 23.7 us -> 20.4 us
    unnamed x4 -> x18, local copies, waits for them, and re-layouts: 2.72 us -> 8.24 us
    pallas_call x1, Pallas kernels: 23.7 us -> 20.4 us  [on_device(): pl.pallas_call(functools.partial(kernel, n, tok, heads, kv_heads, q_soft....]
where the time goes in v2:
time: 29.7 us; the launch traced here: 29.3 us
  Pallas kernels  20.4 us (69%)
  local copies, waits for them, and re-layouts  8.24 us (28%)
  between operations  0.66 us (2%)
    pallas_call x1, Pallas kernels, on_device(): pl.pallas_call(functools.partial(kernel, n, tok, heads, kv_heads, q_soft....  20.4 us
    unnamed x18, local copies, waits for them, and re-layouts  8.24 us

profile of v2, /device:TPU:18, one launch (start us, length us, event | category | flops | bytes accessed | tf_op | source)
XLA Modules:
  0.0 29.3 jit_solution(11599513970132394722)
XLA Ops:
  0.6 0.0 copy-start.6
  0.6 0.0 copy-start.7
  0.7 0.7 %copy-done.6 = f32[256,8]{0,1:T(8,128)S(1)} copy-done((f32[256,8]{0,1:T(8,128)S(1)}, f32[256,8]{0,1:T(8,128)}, u32[]{:S(2)}) %copy-start.6) | copy-done | bytes 8216
  1.3 0.0 copy-done.7
  1.3 0.0 copy-start
  1.3 1.0 %copy-done = bf16[256,8,128]{2,1,0:T(8,128)(2,1)S(1)} copy-done((bf16[256,8,128]{2,1,0:T(8,128)(2,1)S(1)}, bf16[256,8,128]{2,1,0:T(8,128)(2,1)}, u32[]{:S(2)}) %copy-start) | copy-done | bytes 524312
  2.4 0.0 copy-start.1
  2.4 1.0 %copy-done.1 = bf16[256,8,128]{2,1,0:T(8,128)(2,1)S(1)} copy-done((bf16[256,8,128]{2,1,0:T(8,128)(2,1)S(1)}, bf16[256,8,128]{2,1,0:T(8,128)(2,1)}, u32[]{:S(2)}) %copy-start.1) | copy-done | bytes 524312
  3.4 0.0 copy-start.2
  3.4 1.0 %copy-done.2 = bf16[256,8,128]{2,1,0:T(8,128)(2,1)S(1)} copy-done((bf16[256,8,128]{2,1,0:T(8,128)(2,1)S(1)}, bf16[256,8,128]{2,1,0:T(8,128)(2,1)}, u32[]{:S(2)}) %copy-start.2) | copy-done | bytes 524312
  4.5 0.0 copy-start.3
  4.5 1.0 %copy-done.3 = bf16[256,8,128]{2,1,0:T(8,128)(2,1)S(1)} copy-done((bf16[256,8,128]{2,1,0:T(8,128)(2,1)S(1)}, bf16[256,8,128]{2,1,0:T(8,128)(2,1)}, u32[]{:S(2)}) %copy-start.3) | copy-done | bytes 524312
  5.5 0.0 copy-start.4
  5.5 0.9 %copy-done.4 = bf16[256,2,128]{2,1,0:T(2,128)(2,1)S(1)} copy-done((bf16[256,2,128]{2,1,0:T(2,128)(2,1)S(1)}, bf16[256,2,128]{2,1,0:T(2,128)(2,1)}, u32[]{:S(2)}) %copy-start.4) | copy-done | bytes 131096
  6.4 0.0 copy-start.5
  6.4 0.9 %copy-done.5 = bf16[256,2,128]{2,1,0:T(2,128)(2,1)S(1)} copy-done((bf16[256,2,128]{2,1,0:T(2,128)(2,1)S(1)}, bf16[256,2,128]{2,1,0:T(2,128)(2,1)}, u32[]{:S(2)}) %copy-start.5) | copy-done | bytes 131096
  7.3 20.4 %shard_map.95 = (bf16[2048,128]{1,0:T(8,128)(2,1)S(1)}, bf16[2048,128]{1,0:T(8,128)(2,1)S(1)}) custom-call(s32[6]{0:T(128)S(1)} %copy-done.7, bf16[2048,128]{1,0:T(8,128)(2,1)S(1)} %bitcast.11, bf16[2048,128]{1,0:T(8,128)(2,1)S(1)} %bitcast.12, bf16[2048,128]{1,0:T(8,128)(2,1)S(1)} %bitcast.13, f32[8,256]{1,0:T(8,128)S(1)} %bitcast.17, ...), custom_call_target="tpu_custom_call" | custom-call | flops 2000000000 | bytes 4000000 | tf_op jit(solution)/shard_map/pallas_call | solution.py:278
  27.7 0.8 %copy.12 = bf16[256,8,128]{2,1,0:T(8,128)(2,1)} copy(bf16[256,8,128]{2,1,0:T(8,128)(2,1)S(1)} %bitcast.10) | data formatting | bytes 1048576
  28.5 0.8 %copy.13 = bf16[256,8,128]{2,1,0:T(8,128)(2,1)} copy(bf16[256,8,128]{2,1,0:T(8,128)(2,1)S(1)} %bitcast.9) | data formatting | bytes 1048576
Async XLA Ops:
  0.6 0.7 %copy-start.6 = (f32[256,8]{0,1:T(8,128)S(1)}, f32[256,8]{0,1:T(8,128)}, u32[]{:S(2)}) copy-start(f32[256,8]{0,1:T(8,128)} %param.11) | copy-start | bytes 24580
  0.6 0.7 %copy-start.7 = (s32[6]{0:T(128)S(1)}, s32[6]{0:T(128)}, u32[]{:S(2)}) copy-start(s32[6]{0:T(128)} %starts.1) | copy-start | bytes 76
  1.3 1.0 %copy-start = (bf16[256,8,128]{2,1,0:T(8,128)(2,1)S(1)}, bf16[256,8,128]{2,1,0:T(8,128)(2,1)}, u32[]{:S(2)}) copy-start(bf16[256,8,128]{2,1,0:T(8,128)(2,1)} %param.8) | copy-start | bytes 1572868
  2.4 1.0 %copy-start.1 = (bf16[256,8,128]{2,1,0:T(8,128)(2,1)S(1)}, bf16[256,8,128]{2,1,0:T(8,128)(2,1)}, u32[]{:S(2)}) copy-start(bf16[256,8,128]{2,1,0:T(8,128)(2,1)} %param.9) | copy-start | bytes 1572868
  3.4 1.0 %copy-start.2 = (bf16[256,8,128]{2,1,0:T(8,128)(2,1)S(1)}, bf16[256,8,128]{2,1,0:T(8,128)(2,1)}, u32[]{:S(2)}) copy-start(bf16[256,8,128]{2,1,0:T(8,128)(2,1)} %param.10) | copy-start | bytes 1572868
  4.5 1.0 %copy-start.3 = (bf16[256,8,128]{2,1,0:T(8,128)(2,1)S(1)}, bf16[256,8,128]{2,1,0:T(8,128)(2,1)}, u32[]{:S(2)}) copy-start(bf16[256,8,128]{2,1,0:T(8,128)(2,1)} %param.12) | copy-start | bytes 1572868
  5.5 0.9 %copy-start.4 = (bf16[256,2,128]{2,1,0:T(2,128)(2,1)S(1)}, bf16[256,2,128]{2,1,0:T(2,128)(2,1)}, u32[]{:S(2)}) copy-start(bf16[256,2,128]{2,1,0:T(2,128)(2,1)} %param.13) | copy-start | bytes 393220
  6.4 0.9 %copy-start.5 = (bf16[256,2,128]{2,1,0:T(2,128)(2,1)S(1)}, bf16[256,2,128]{2,1,0:T(2,128)(2,1)}, u32[]{:S(2)}) copy-start(bf16[256,2,128]{2,1,0:T(2,128)(2,1)} %param.14) | copy-start | bytes 393220
